TPU v7x, 256 devices: a whole 4x4x8 slice. The times are simulated.
256 devices in a mesh: ctx: 16 (over y_hi, x, core), smp: 16 (over y_lo, z).
Axes of the slice: x: 4, y: 4 (y_hi: 2, y_lo: 2; y = y_hi * 2 + y_lo), z: 8, core: 2. Of those that a mesh axis runs over, the one named last changes fastest.
Arguments:
- hidden_states: bfloat16 [64, 64, 5120], P('smp'), may hold values from -6 to 6
- query_weight: bfloat16 [5120, 5120], P('smp', 'ctx'), may hold values from -0.078125 to 0.078125
- kv_weight: bfloat16 [5120, 2048], P('smp', 'ctx'), may hold values from -0.078125 to 0.078125
- out_weight: bfloat16 [5120, 5120], P('smp', 'ctx'), may hold values from -0.078125 to 0.078125
- query_bias: bfloat16 [5120], P('ctx'), may hold values from -3 to 3
- kv_bias: bfloat16 [2048], P('ctx'), may hold values from -3 to 3
- prompt_kv: bfloat16 [4096, 2, 1024], P('ctx')
- parents: int32 [64, 64], P('smp'), may hold values from 0 to 62, as said below
- prefix_len: int32 [64], P('smp'), may hold values from 1024 to 4096, as said below
Outputs:
- layer_out: float32 [64, 64, 5120], P('smp', None, 'ctx')
Inputs may be any that keep to these rules, and one draw needn't show every extreme that they name: parents[s, 0] = 0, and for n >= 1 the parent of node n is an earlier node. `prefix_len`: some sample sees the whole prompt.
All inputs are finite; a program needn't handle non-finite values.
Results may differ from a plain program's by a relative error of at most 0.009.
The roundings to bfloat16 on the way count: a program that leaves them out, or rounds other values in their place, can miss the bound.
Values may be sent and summed in bfloat16 or wider, within the bound.
A program may use at most 64 MiB of HBM per device.

v0:
```python
import jax
import jax.numpy as jnp
from jax import lax
from jax.sharding import PartitionSpec as P

HQ = 40
KVH = 8
HD = 128
NODES = 64
SMP_DEV = 4
PROMPT_DEV = 256


rope_theta = 1000000.0
neg_big = -1e30


def passed_along(block, axis, distance):
    devices = range(lax.axis_size(axis))
    route = [((i - distance) % len(devices), i) for i in devices]
    return lax.ppermute(block, axis, route)


def ancestors(parents):
    node_count = parents.shape[-1]
    node_ids = jnp.arange(node_count, dtype=jnp.int32)
    step_up = (parents[..., :, None] == node_ids[None, None, :]).astype(jnp.float32)
    step_up = step_up * (node_ids[:, None] > 0).astype(jnp.float32)[None]
    reach = step_up + jnp.eye(node_count, dtype=jnp.float32)[None]
    for squaring in range(max(node_count - 1, 1).bit_length()):
        reach = jnp.minimum(
            jnp.einsum("snm,smk->snk", reach, reach, precision=lax.Precision.HIGHEST), 1.0
        )
    return reach


def rotate(values, positions):
    midpoint = values.shape[-1] // 2
    frequency = rope_theta ** (-jnp.arange(midpoint, dtype=jnp.float32) / midpoint)
    angles = positions[:, None] * frequency[None, :]
    cosine = jnp.cos(angles)[:, None, :]
    sine_part = jnp.sin(angles)[:, None, :]
    lower_half = values[..., :midpoint]
    upper_half = values[..., midpoint:]
    return jnp.concatenate(
        [
            lower_half * cosine - upper_half * sine_part,
            upper_half * cosine + lower_half * sine_part,
        ],
        axis=-1,
    )


def empty_state(row_count, heads_here, group):
    return (
        jnp.full((row_count, heads_here, group), neg_big, jnp.float32),
        jnp.zeros((row_count, heads_here, group), jnp.float32),
        jnp.zeros((row_count, heads_here, group, HD), jnp.float32),
    )


def attend_block(state, queries, keys, values, allowed):
    running_max, running_sum, running_acc = state
    scores = jnp.einsum(
        "rkgd,pkd->rkgp", queries, keys, preferred_element_type=jnp.float32
    ) * HD ** (-0.5)
    wide_mask = allowed[:, None, None, :]
    scores = jnp.where(wide_mask, scores, neg_big)
    new_max = jnp.maximum(running_max, jnp.max(scores, axis=-1))
    weights = jnp.where(wide_mask, jnp.exp(scores - new_max[..., None]), 0.0)
    factor = jnp.exp(running_max - new_max)
    new_sum = running_sum * factor + jnp.sum(weights, axis=-1)
    product = jnp.einsum(
        "rkgp,pkd->rkgd", weights.astype(jnp.bfloat16), values, preferred_element_type=jnp.float32
    )
    return (new_max, new_sum, running_acc * factor[..., None] + product)


def split_block(block):
    heads_here = block.shape[2] // HD
    return (
        block[:, 0].reshape(block.shape[0], heads_here, HD),
        block[:, 1].reshape(block.shape[0], heads_here, HD),
    )


def visible(row_limits, anchor):
    key_pos = anchor * PROMPT_DEV + jnp.arange(PROMPT_DEV, dtype=jnp.int32)
    return key_pos[None, :] < row_limits[:, None]


def shards(
    hidden_states,
    query_weight,
    kv_weight,
    out_weight,
    query_bias,
    kv_bias,
    prompt_kv,
    parents,
    prefix_len,
):
    group = HQ // KVH
    ctx_size = lax.axis_size("ctx")
    ctx_index = lax.axis_index("ctx")
    tree_rows = SMP_DEV * NODES
    own_rows = tree_rows // ctx_size
    row_start = ctx_index * own_rows
    flat = hidden_states.reshape(tree_rows, hidden_states.shape[2])
    columns = flat
    query_part = jnp.dot(
        columns,
        lax.all_gather(query_weight, "smp", axis=0, tiled=True),
        preferred_element_type=jnp.float32,
    )
    kv_part = jnp.dot(
        columns,
        lax.all_gather(kv_weight, "smp", axis=0, tiled=True),
        preferred_element_type=jnp.float32,
    )
    query_part = (query_part + query_bias[None, :].astype(jnp.float32)).astype(jnp.bfloat16)
    kv_part = (kv_part + kv_bias[None, :].astype(jnp.float32)).astype(jnp.bfloat16)
    query_lin = lax.all_to_all(query_part, "ctx", split_axis=0, concat_axis=1, tiled=True)
    tree_kv = lax.all_gather(kv_part, "ctx", axis=1, tiled=True)
    reach = ancestors(parents)
    positions = (prefix_len.astype(jnp.float32)[:, None] + jnp.sum(reach, axis=-1) - 1.0).reshape(
        tree_rows
    )
    tree_keys = rotate(
        tree_kv[:, : KVH * HD].astype(jnp.float32).reshape(tree_rows, KVH, HD), positions
    ).astype(jnp.bfloat16)
    tree_values = tree_kv[:, KVH * HD :].reshape(tree_rows, KVH, HD)
    own_positions = lax.dynamic_slice_in_dim(positions, row_start, own_rows)
    queries = rotate(query_lin.astype(jnp.float32).reshape(own_rows, HQ, HD), own_positions).astype(
        jnp.bfloat16
    )
    queries = queries.reshape(own_rows, KVH, group, HD)
    row_ids = row_start + jnp.arange(own_rows, dtype=jnp.int32)
    key_ids = jnp.arange(tree_rows, dtype=jnp.int32)
    reach_rows = lax.dynamic_slice_in_dim(reach.reshape(tree_rows, NODES), row_start, own_rows)
    same_sample = row_ids[:, None] // NODES == key_ids[None, :] // NODES
    tree_allowed = same_sample & (jnp.tile(reach_rows, (1, SMP_DEV)) > 0.5)
    every_limit = jnp.repeat(prefix_len, NODES)
    limits = lax.dynamic_slice_in_dim(every_limit, row_start, own_rows)
    tree_state = attend_block(
        empty_state(own_rows, KVH, group), queries, tree_keys, tree_values, tree_allowed
    )
    local_keys, local_values = split_block(prompt_kv)
    state = attend_block(tree_state, queries, local_keys, local_values, visible(limits, ctx_index))

    def turn(step, carry):
        block, running = carry
        block = passed_along(block, "ctx", 1)
        anchor = (ctx_index - step) % ctx_size
        block_keys, block_values = split_block(block)
        return (
            block,
            attend_block(running, queries, block_keys, block_values, visible(limits, anchor)),
        )

    state = lax.fori_loop(1, ctx_size, turn, (prompt_kv, state))[1]
    attn = (state[2] / state[1][..., None]).astype(jnp.bfloat16).reshape(own_rows, HQ * HD)
    every_row = lax.all_gather(attn, "ctx", axis=0, tiled=True)
    columns = every_row
    result = jnp.dot(
        columns,
        lax.all_gather(out_weight, "smp", axis=0, tiled=True),
        preferred_element_type=jnp.float32,
    )
    return result.reshape(SMP_DEV, NODES, out_weight.shape[1])


def solution(mesh):
    return jax.shard_map(
        shards,
        mesh=mesh,
        in_specs=(
            P("smp", None, None),
            P("smp", "ctx"),
            P("smp", "ctx"),
            P("smp", "ctx"),
            P("ctx"),
            P("ctx"),
            P("ctx", None, None),
            P("smp", None),
            P("smp"),
        ),
        out_specs=P("smp", None, "ctx"),
        check_vma=False,
    )
```

profile of v0, /device:TPU:1, one launch (start us, length us, event | category | flops | bytes accessed | tf_op | source)
XLA Modules:
  0.0 659.3 jit_solution(6417092861920433570)
XLA Ops:
  8.0 65.1 %all-gather.6.cloned.1.call-done = bf16[5120,128]{1,0:T(8,128)(2,1)} async-done(((bf16[320,128]{1,0:T(8,128)(2,1)}), bf16[5120,128]{1,0:T(8,128)(2,1)}) %all-gather.6.cloned.1.call-update) | async-done | bytes 1310736 | tf_op jit(solution)/shard_map/all_gather | solution.py:118
  73.1 2.8 fusion.18
  81.1 3.6 copy.51
  84.8 2.2 fusion.48
  87.1 47.1 %all-gather.8.cloned.1.call-done = bf16[256,2048]{1,0:T(8,128)(2,1)} async-done(((bf16[256,128]{1,0:T(8,128)(2,1)}), bf16[256,2048]{1,0:T(8,128)(2,1)}) %all-gather.8.cloned.1.call-update) | async-done | bytes 1048592 | tf_op jit(solution)/shard_map/all_gather | solution.py:124
  134.2 1.3 slice_bitcast_fusion
  135.7 1.6 fusion.49
  137.4 64.6 %all-gather.10.cloned.1.call-done = bf16[5120,320]{1,0:T(8,128)(2,1)} async-done(((bf16[320,320]{1,0:T(8,128)(2,1)}), bf16[5120,320]{1,0:T(8,128)(2,1)}) %all-gather.10.cloned.1.call-update) | async-done | bytes 3276816 | tf_op jit(solution)/shard_map/all_gather | solution.py:113
  202.0 3.7 fusion.17
  206.5 15.8 %all-to-all-start = ((bf16[16,16,320]{2,1,0:T(8,128)(2,1)}), bf16[16,16,320]{2,1,0:T(8,128)(2,1)}, u32[]{:S(2)}, u32[]{:S(2)}) async-start(bf16[16,16,320]{2,1,0:T(8,128)(2,1)} %bitcast.10), calls=%async_computation | async-start | bytes 393216 | tf_op jit(solution)/shard_map/all_to_all | solution.py:123
  222.5 2.9 subtract_convert_fusion
  226.4 8.1 %all-to-all-done = bf16[16,16,320]{2,1,0:T(8,128)(2,1)} async-done(((bf16[16,16,320]{2,1,0:T(8,128)(2,1)}), bf16[16,16,320]{2,1,0:T(8,128)(2,1)}, u32[]{:S(2)}, u32[]{:S(2)}) %all-to-all-start) | async-done | bytes 163872 | tf_op jit(solution)/shard_map/all_to_all | solution.py:123
  236.3 1.2 reshape.373
  240.5 341.6 %while.21 = (s32[]{:T(128)}, bf16[256,2,1024]{0,2,1:T(8,128)(2,1)}, f32[16,8,5]{0,2,1:T(8,128)S(1)}, f32[16,8,5]{0,2,1:T(8,128)S(1)}, f32[16,8,5,128]{3,0,2,1:T(...) while((s32[]{:T(128)}, bf16[256,2,1024]{0,2,1:T(8,128)(2,1)}, ...), condition=%wide.region_8.9_spmd, body=%wide.region_5.8_spmd.sunk | while | flops 85530128 | bytes 12282222 | solution.py:161
  240.5 1.6 collective-permute-start
  242.2 12.0 %collective-permute-done = bf16[256,2,1024]{0,2,1:T(8,128)(2,1)} collective-permute-done((bf16[256,2,1024]{0,2,1:T(8,128)(2,1)}, bf16[256,2,1024]{0,2,1:T(8,128)(2,1)}, u32[]{:S(2)}, u32[]{:S(2)}) %collective-permute-start) | collective-permute-done | bytes 1048608 | tf_op jit(solution)/shard_map/while/body/eval_jaxpr/ppermute | solution.py:21
  254.1 1.3 fusion.89
  256.5 2.3 copy.95
  258.8 2.5 collective-permute-start
  261.4 12.0 %collective-permute-done = bf16[256,2,1024]{0,2,1:T(8,128)(2,1)} collective-permute-done((bf16[256,2,1024]{0,2,1:T(8,128)(2,1)}, bf16[256,2,1024]{0,2,1:T(8,128)(2,1)}, u32[]{:S(2)}, u32[]{:S(2)}) %collective-permute-start) | collective-permute-done | bytes 1048608 | tf_op jit(solution)/shard_map/while/body/eval_jaxpr/ppermute | solution.py:21
  273.4 1.3 fusion.89
  275.7 2.3 copy.95
  278.1 2.5 collective-permute-start
  280.6 22.8 %collective-permute-done = bf16[256,2,1024]{0,2,1:T(8,128)(2,1)} collective-permute-done((bf16[256,2,1024]{0,2,1:T(8,128)(2,1)}, bf16[256,2,1024]{0,2,1:T(8,128)(2,1)}, u32[]{:S(2)}, u32[]{:S(2)}) %collective-permute-start) | collective-permute-done | bytes 1048608 | tf_op jit(solution)/shard_map/while/body/eval_jaxpr/ppermute | solution.py:21
  303.4 1.3 fusion.89
  305.7 2.3 copy.95
  308.2 18.1 %collective-permute-done = bf16[256,2,1024]{0,2,1:T(8,128)(2,1)} collective-permute-done((bf16[256,2,1024]{0,2,1:T(8,128)(2,1)}, bf16[256,2,1024]{0,2,1:T(8,128)(2,1)}, u32[]{:S(2)}, u32[]{:S(2)}) %collective-permute-start) | collective-permute-done | bytes 1048608 | tf_op jit(solution)/shard_map/while/body/eval_jaxpr/ppermute | solution.py:21
  326.2 1.3 fusion.89
  328.6 2.3 copy.95
  331.0 18.1 %collective-permute-done = bf16[256,2,1024]{0,2,1:T(8,128)(2,1)} collective-permute-done((bf16[256,2,1024]{0,2,1:T(8,128)(2,1)}, bf16[256,2,1024]{0,2,1:T(8,128)(2,1)}, u32[]{:S(2)}, u32[]{:S(2)}) %collective-permute-start) | collective-permute-done | bytes 1048608 | tf_op jit(solution)/shard_map/while/body/eval_jaxpr/ppermute | solution.py:21
  349.1 1.3 fusion.89
  351.4 2.3 copy.95
  353.8 18.1 %collective-permute-done = bf16[256,2,1024]{0,2,1:T(8,128)(2,1)} collective-permute-done((bf16[256,2,1024]{0,2,1:T(8,128)(2,1)}, bf16[256,2,1024]{0,2,1:T(8,128)(2,1)}, u32[]{:S(2)}, u32[]{:S(2)}) %collective-permute-start) | collective-permute-done | bytes 1048608 | tf_op jit(solution)/shard_map/while/body/eval_jaxpr/ppermute | solution.py:21
  371.9 1.3 fusion.89
  374.2 2.3 copy.95
  376.7 18.1 %collective-permute-done = bf16[256,2,1024]{0,2,1:T(8,128)(2,1)} collective-permute-done((bf16[256,2,1024]{0,2,1:T(8,128)(2,1)}, bf16[256,2,1024]{0,2,1:T(8,128)(2,1)}, u32[]{:S(2)}, u32[]{:S(2)}) %collective-permute-start) | collective-permute-done | bytes 1048608 | tf_op jit(solution)/shard_map/while/body/eval_jaxpr/ppermute | solution.py:21
  394.7 1.3 fusion.89
  397.1 2.3 copy.95
  399.5 18.1 %collective-permute-done = bf16[256,2,1024]{0,2,1:T(8,128)(2,1)} collective-permute-done((bf16[256,2,1024]{0,2,1:T(8,128)(2,1)}, bf16[256,2,1024]{0,2,1:T(8,128)(2,1)}, u32[]{:S(2)}, u32[]{:S(2)}) %collective-permute-start) | collective-permute-done | bytes 1048608 | tf_op jit(solution)/shard_map/while/body/eval_jaxpr/ppermute | solution.py:21
  417.6 1.3 fusion.89
  419.9 2.3 copy.95
  422.3 18.1 %collective-permute-done = bf16[256,2,1024]{0,2,1:T(8,128)(2,1)} collective-permute-done((bf16[256,2,1024]{0,2,1:T(8,128)(2,1)}, bf16[256,2,1024]{0,2,1:T(8,128)(2,1)}, u32[]{:S(2)}, u32[]{:S(2)}) %collective-permute-start) | collective-permute-done | bytes 1048608 | tf_op jit(solution)/shard_map/while/body/eval_jaxpr/ppermute | solution.py:21
  440.4 1.3 fusion.89
  442.8 2.3 copy.95
  445.2 18.1 %collective-permute-done = bf16[256,2,1024]{0,2,1:T(8,128)(2,1)} collective-permute-done((bf16[256,2,1024]{0,2,1:T(8,128)(2,1)}, bf16[256,2,1024]{0,2,1:T(8,128)(2,1)}, u32[]{:S(2)}, u32[]{:S(2)}) %collective-permute-start) | collective-permute-done | bytes 1048608 | tf_op jit(solution)/shard_map/while/body/eval_jaxpr/ppermute | solution.py:21
  463.2 1.3 fusion.89
  465.6 2.3 copy.95
  468.0 18.1 %collective-permute-done = bf16[256,2,1024]{0,2,1:T(8,128)(2,1)} collective-permute-done((bf16[256,2,1024]{0,2,1:T(8,128)(2,1)}, bf16[256,2,1024]{0,2,1:T(8,128)(2,1)}, u32[]{:S(2)}, u32[]{:S(2)}) %collective-permute-start) | collective-permute-done | bytes 1048608 | tf_op jit(solution)/shard_map/while/body/eval_jaxpr/ppermute | solution.py:21
  486.1 1.3 fusion.89
  488.4 2.3 copy.95
  490.9 18.1 %collective-permute-done = bf16[256,2,1024]{0,2,1:T(8,128)(2,1)} collective-permute-done((bf16[256,2,1024]{0,2,1:T(8,128)(2,1)}, bf16[256,2,1024]{0,2,1:T(8,128)(2,1)}, u32[]{:S(2)}, u32[]{:S(2)}) %collective-permute-start) | collective-permute-done | bytes 1048608 | tf_op jit(solution)/shard_map/while/body/eval_jaxpr/ppermute | solution.py:21
  508.9 1.3 fusion.89
  511.3 2.3 copy.95
  513.7 18.1 %collective-permute-done = bf16[256,2,1024]{0,2,1:T(8,128)(2,1)} collective-permute-done((bf16[256,2,1024]{0,2,1:T(8,128)(2,1)}, bf16[256,2,1024]{0,2,1:T(8,128)(2,1)}, u32[]{:S(2)}, u32[]{:S(2)}) %collective-permute-start) | collective-permute-done | bytes 1048608 | tf_op jit(solution)/shard_map/while/body/eval_jaxpr/ppermute | solution.py:21
  531.8 1.3 fusion.89
  534.1 2.3 copy.95
  536.5 18.1 %collective-permute-done = bf16[256,2,1024]{0,2,1:T(8,128)(2,1)} collective-permute-done((bf16[256,2,1024]{0,2,1:T(8,128)(2,1)}, bf16[256,2,1024]{0,2,1:T(8,128)(2,1)}, u32[]{:S(2)}, u32[]{:S(2)}) %collective-permute-start) | collective-permute-done | bytes 1048608 | tf_op jit(solution)/shard_map/while/body/eval_jaxpr/ppermute | solution.py:21
  554.6 1.3 fusion.89
  557.0 2.3 copy.95
  559.4 18.1 %collective-permute-done = bf16[256,2,1024]{0,2,1:T(8,128)(2,1)} collective-permute-done((bf16[256,2,1024]{0,2,1:T(8,128)(2,1)}, bf16[256,2,1024]{0,2,1:T(8,128)(2,1)}, u32[]{:S(2)}, u32[]{:S(2)}) %collective-permute-start) | collective-permute-done | bytes 1048608 | tf_op jit(solution)/shard_map/while/body/eval_jaxpr/ppermute | solution.py:21
  577.4 1.3 fusion.89
  579.8 2.3 copy.95
  583.3 64.3 %all-gather.12.cloned.1.call-done = bf16[256,5120]{1,0:T(8,128)(2,1)} async-done(((bf16[16,5120]{1,0:T(8,128)(2,1)}), bf16[256,5120]{1,0:T(8,128)(2,1)}) %all-gather.12.cloned.1.call-update) | async-done | bytes 2621456 | tf_op jit(solution)/shard_map/all_gather | solution.py:163
  647.6 5.2 fusion.53
  (208 shorter events, 31.4 us)
Async XLA Ops:
  6.5 66.6 %copy-start = (bf16[4,64,5120]{2,1,0:T(8,128)(2,1)S(1)}, bf16[4,64,5120]{2,1,0:T(8,128)(2,1)}, u32[]{:S(2)}) copy-start(bf16[4,64,5120]{2,1,0:T(8,128)(2,1)} %param.11) | copy-start | bytes 7864324
  6.5 70.8 %copy-start.8 = (s32[4,64]{1,0:T(4,128)S(1)}, s32[4,64]{1,0:T(4,128)}, u32[]{:S(2)}) copy-start(s32[4,64]{1,0:T(4,128)} %param.18) | copy-start | bytes 3076
  6.5 66.6 %all-gather.6.cloned.1.call-start = ((), (), s32[]{:S(2)}) async-start(), calls=%async_computation.1 | async-start | bytes 1392640 | tf_op jit(solution)/shard_map/all_gather | solution.py:118
  7.3 126.9 %all-gather.8.cloned.1.call-start = ((), (), s32[]{:S(2)}) async-start(), calls=%async_computation.2 | async-start | bytes 1114112 | tf_op jit(solution)/shard_map/all_gather | solution.py:124
  73.1 6.0 copy-start.7
  73.1 7.6 %copy-start.6 = (bf16[320]{0:T(512)(128)(2,1)S(1)}, bf16[320]{0:T(512)(128)(2,1)}, u32[]{:S(2)}) copy-start(bf16[320]{0:T(512)(128)(2,1)} %param.15) | copy-start | bytes 1924
  76.0 126.0 %all-gather.10.cloned.1.call-start = ((), (), s32[]{:S(2)}) async-start(), calls=%async_computation.3 | async-start | bytes 4177920 | tf_op jit(solution)/shard_map/all_gather | solution.py:113
  76.7 506.6 %all-gather.14.cloned.1.call-start = ((), (), s32[]{:S(2)}) async-start(), calls=%async_computation.5 | async-start | bytes 4177920 | tf_op jit(solution)/shard_map/all_gather | solution.py:167
  206.5 28.0 %all-to-all-start = ((bf16[16,16,320]{2,1,0:T(8,128)(2,1)}), bf16[16,16,320]{2,1,0:T(8,128)(2,1)}, u32[]{:S(2)}, u32[]{:S(2)}) async-start(bf16[16,16,320]{2,1,0:T(8,128)(2,1)} %bitcast.10), calls=%async_computation | async-start | bytes 393216 | tf_op jit(solution)/shard_map/all_to_all | solution.py:123
  222.3 425.3 %all-gather.12.cloned.1.call-start = ((), (), s32[]{:S(2)}) async-start(), calls=%async_computation.4 | async-start | bytes 2785280 | tf_op jit(solution)/shard_map/all_gather | solution.py:163
  226.4 11.5 %copy-start.2 = (bf16[256,1,1024]{0,2,1:T(8,128)(2,1)S(1)}, bf16[256,1,1024]{0,2,1:T(8,128)(2,1)}, u32[]{:S(2)}) copy-start(bf16[256,1,1024]{0,2,1:T(8,128)(2,1)} %get-tuple-element.250) | copy-start | bytes 1572868
  237.5 1.0 copy-start.3
  237.5 1.2 copy-start.4
  237.9 1.9 copy-start.5
  238.7 1.4 copy-start.1
  240.5 13.6 %collective-permute-start = (bf16[256,2,1024]{0,2,1:T(8,128)(2,1)}, bf16[256,2,1024]{0,2,1:T(8,128)(2,1)}, u32[]{:S(2)}, u32[]{:S(2)}) collective-permute-start(bf16[256,2,1024]{0,2,1:T(8,128)(2,1)} %get-tuple-element.347), channel_id=1, source_target_pairs={{240,0},{0,16},{16,32},{32,48},{48,64},{64,80},{80,96},{96,112},{1... | collective-permute-start | bytes 3145736 | tf_op jit(solution)/shard_map/while/body/eval_jaxpr/ppermute | solution.py:21
  258.8 14.5 %collective-permute-start = (bf16[256,2,1024]{0,2,1:T(8,128)(2,1)}, bf16[256,2,1024]{0,2,1:T(8,128)(2,1)}, u32[]{:S(2)}, u32[]{:S(2)}) collective-permute-start(bf16[256,2,1024]{0,2,1:T(8,128)(2,1)} %get-tuple-element.347), channel_id=1, source_target_pairs={{240,0},{0,16},{16,32},{32,48},{48,64},{64,80},{80,96},{96,112},{1... | collective-permute-start | bytes 3145736 | tf_op jit(solution)/shard_map/while/body/eval_jaxpr/ppermute | solution.py:21
  278.1 25.3 %collective-permute-start = (bf16[256,2,1024]{0,2,1:T(8,128)(2,1)}, bf16[256,2,1024]{0,2,1:T(8,128)(2,1)}, u32[]{:S(2)}, u32[]{:S(2)}) collective-permute-start(bf16[256,2,1024]{0,2,1:T(8,128)(2,1)} %get-tuple-element.347), channel_id=1, source_target_pairs={{240,0},{0,16},{16,32},{32,48},{48,64},{64,80},{80,96},{96,112},{1... | collective-permute-start | bytes 3145736 | tf_op jit(solution)/shard_map/while/body/eval_jaxpr/ppermute | solution.py:21
  308.1 18.2 %collective-permute-start = (bf16[256,2,1024]{0,2,1:T(8,128)(2,1)}, bf16[256,2,1024]{0,2,1:T(8,128)(2,1)}, u32[]{:S(2)}, u32[]{:S(2)}) collective-permute-start(bf16[256,2,1024]{0,2,1:T(8,128)(2,1)} %get-tuple-element.347), channel_id=1, source_target_pairs={{240,0},{0,16},{16,32},{32,48},{48,64},{64,80},{80,96},{96,112},{1... | collective-permute-start | bytes 3145736 | tf_op jit(solution)/shard_map/while/body/eval_jaxpr/ppermute | solution.py:21
  330.9 18.2 %collective-permute-start = (bf16[256,2,1024]{0,2,1:T(8,128)(2,1)}, bf16[256,2,1024]{0,2,1:T(8,128)(2,1)}, u32[]{:S(2)}, u32[]{:S(2)}) collective-permute-start(bf16[256,2,1024]{0,2,1:T(8,128)(2,1)} %get-tuple-element.347), channel_id=1, source_target_pairs={{240,0},{0,16},{16,32},{32,48},{48,64},{64,80},{80,96},{96,112},{1... | collective-permute-start | bytes 3145736 | tf_op jit(solution)/shard_map/while/body/eval_jaxpr/ppermute | solution.py:21
  353.7 18.2 %collective-permute-start = (bf16[256,2,1024]{0,2,1:T(8,128)(2,1)}, bf16[256,2,1024]{0,2,1:T(8,128)(2,1)}, u32[]{:S(2)}, u32[]{:S(2)}) collective-permute-start(bf16[256,2,1024]{0,2,1:T(8,128)(2,1)} %get-tuple-element.347), channel_id=1, source_target_pairs={{240,0},{0,16},{16,32},{32,48},{48,64},{64,80},{80,96},{96,112},{1... | collective-permute-start | bytes 3145736 | tf_op jit(solution)/shard_map/while/body/eval_jaxpr/ppermute | solution.py:21
  376.6 18.2 %collective-permute-start = (bf16[256,2,1024]{0,2,1:T(8,128)(2,1)}, bf16[256,2,1024]{0,2,1:T(8,128)(2,1)}, u32[]{:S(2)}, u32[]{:S(2)}) collective-permute-start(bf16[256,2,1024]{0,2,1:T(8,128)(2,1)} %get-tuple-element.347), channel_id=1, source_target_pairs={{240,0},{0,16},{16,32},{32,48},{48,64},{64,80},{80,96},{96,112},{1... | collective-permute-start | bytes 3145736 | tf_op jit(solution)/shard_map/while/body/eval_jaxpr/ppermute | solution.py:21
  399.4 18.2 %collective-permute-start = (bf16[256,2,1024]{0,2,1:T(8,128)(2,1)}, bf16[256,2,1024]{0,2,1:T(8,128)(2,1)}, u32[]{:S(2)}, u32[]{:S(2)}) collective-permute-start(bf16[256,2,1024]{0,2,1:T(8,128)(2,1)} %get-tuple-element.347), channel_id=1, source_target_pairs={{240,0},{0,16},{16,32},{32,48},{48,64},{64,80},{80,96},{96,112},{1... | collective-permute-start | bytes 3145736 | tf_op jit(solution)/shard_map/while/body/eval_jaxpr/ppermute | solution.py:21
  422.3 18.2 %collective-permute-start = (bf16[256,2,1024]{0,2,1:T(8,128)(2,1)}, bf16[256,2,1024]{0,2,1:T(8,128)(2,1)}, u32[]{:S(2)}, u32[]{:S(2)}) collective-permute-start(bf16[256,2,1024]{0,2,1:T(8,128)(2,1)} %get-tuple-element.347), channel_id=1, source_target_pairs={{240,0},{0,16},{16,32},{32,48},{48,64},{64,80},{80,96},{96,112},{1... | collective-permute-start | bytes 3145736 | tf_op jit(solution)/shard_map/while/body/eval_jaxpr/ppermute | solution.py:21
  445.1 18.2 %collective-permute-start = (bf16[256,2,1024]{0,2,1:T(8,128)(2,1)}, bf16[256,2,1024]{0,2,1:T(8,128)(2,1)}, u32[]{:S(2)}, u32[]{:S(2)}) collective-permute-start(bf16[256,2,1024]{0,2,1:T(8,128)(2,1)} %get-tuple-element.347), channel_id=1, source_target_pairs={{240,0},{0,16},{16,32},{32,48},{48,64},{64,80},{80,96},{96,112},{1... | collective-permute-start | bytes 3145736 | tf_op jit(solution)/shard_map/while/body/eval_jaxpr/ppermute | solution.py:21
  467.9 18.2 %collective-permute-start = (bf16[256,2,1024]{0,2,1:T(8,128)(2,1)}, bf16[256,2,1024]{0,2,1:T(8,128)(2,1)}, u32[]{:S(2)}, u32[]{:S(2)}) collective-permute-start(bf16[256,2,1024]{0,2,1:T(8,128)(2,1)} %get-tuple-element.347), channel_id=1, source_target_pairs={{240,0},{0,16},{16,32},{32,48},{48,64},{64,80},{80,96},{96,112},{1... | collective-permute-start | bytes 3145736 | tf_op jit(solution)/shard_map/while/body/eval_jaxpr/ppermute | solution.py:21
  490.8 18.2 %collective-permute-start = (bf16[256,2,1024]{0,2,1:T(8,128)(2,1)}, bf16[256,2,1024]{0,2,1:T(8,128)(2,1)}, u32[]{:S(2)}, u32[]{:S(2)}) collective-permute-start(bf16[256,2,1024]{0,2,1:T(8,128)(2,1)} %get-tuple-element.347), channel_id=1, source_target_pairs={{240,0},{0,16},{16,32},{32,48},{48,64},{64,80},{80,96},{96,112},{1... | collective-permute-start | bytes 3145736 | tf_op jit(solution)/shard_map/while/body/eval_jaxpr/ppermute | solution.py:21
  513.6 18.2 %collective-permute-start = (bf16[256,2,1024]{0,2,1:T(8,128)(2,1)}, bf16[256,2,1024]{0,2,1:T(8,128)(2,1)}, u32[]{:S(2)}, u32[]{:S(2)}) collective-permute-start(bf16[256,2,1024]{0,2,1:T(8,128)(2,1)} %get-tuple-element.347), channel_id=1, source_target_pairs={{240,0},{0,16},{16,32},{32,48},{48,64},{64,80},{80,96},{96,112},{1... | collective-permute-start | bytes 3145736 | tf_op jit(solution)/shard_map/while/body/eval_jaxpr/ppermute | solution.py:21
  536.4 18.2 %collective-permute-start = (bf16[256,2,1024]{0,2,1:T(8,128)(2,1)}, bf16[256,2,1024]{0,2,1:T(8,128)(2,1)}, u32[]{:S(2)}, u32[]{:S(2)}) collective-permute-start(bf16[256,2,1024]{0,2,1:T(8,128)(2,1)} %get-tuple-element.347), channel_id=1, source_target_pairs={{240,0},{0,16},{16,32},{32,48},{48,64},{64,80},{80,96},{96,112},{1... | collective-permute-start | bytes 3145736 | tf_op jit(solution)/shard_map/while/body/eval_jaxpr/ppermute | solution.py:21
  559.3 18.2 %collective-permute-start = (bf16[256,2,1024]{0,2,1:T(8,128)(2,1)}, bf16[256,2,1024]{0,2,1:T(8,128)(2,1)}, u32[]{:S(2)}, u32[]{:S(2)}) collective-permute-start(bf16[256,2,1024]{0,2,1:T(8,128)(2,1)} %get-tuple-element.347), channel_id=1, source_target_pairs={{240,0},{0,16},{16,32},{32,48},{48,64},{64,80},{80,96},{96,112},{1... | collective-permute-start | bytes 3145736 | tf_op jit(solution)/shard_map/while/body/eval_jaxpr/ppermute | solution.py:21
Sparse Core Ops, SparseCore 0:
  9.1 63.9 all-gather.5
  76.1 58.0 all-gather.7
  136.0 65.9 all-gather.9
  203.6 85.2 all-gather.13
  583.4 64.1 all-gather.11
where the time goes:
time: 661 us; the launch traced here: 659 us
  waiting for transfers between devices  515 us (78%)
  local copies, waits for them, and re-layouts  67.6 us (10%)
  matrix products  25.5 us (4%)
  starting transfers between devices  22.7 us (3%)
  other arithmetic  14.6 us (2%)
  between operations  13.5 us (2%)
    ppermute x15, waiting for transfers between devices, passed_along(): return lax.ppermute(block, axis, route)  264 us
    all_gather x1, waiting for transfers between devices, shards(): lax.all_gather(kv_weight, 'smp', axis=0, tiled=True)  65.1 us
    all_gather x1, waiting for transfers between devices, shards(): lax.all_gather(query_weight, 'smp', axis=0, tiled=True)  64.6 us
    all_gather x1, waiting for transfers between devices, shards(): every_row = lax.all_gather(attn, 'ctx', axis=0, tiled=True)  64.3 us
    all_gather x1, waiting for transfers between devices, shards(): tree_kv = lax.all_gather(kv_part, 'ctx', axis=1, tiled=True)  47.1 us
    while x30, local copies, waits for them, and re-layouts  35.1 us
    slice x16, local copies, waits for them, and re-layouts, split_block(): block[:, 1].reshape(block.shape[0], heads_here, HD)  21.3 us
    all_to_all x1, starting transfers between devices, shards(): lax.all_to_all(query_part, 'ctx', split_axis=0, concat_axis=1, tiled=True)  15.8 us
  transfers between devices with their start and end apart: 21, of which 20 were waited for; matrix products, arithmetic and copies ran while one was open for 15% of the time, Pallas kernels for 0%

commit v1 on v0

v1 whole, which is shorter than its diff:
```python
import functools

import jax
import jax.numpy as jnp
from jax import lax
from jax.experimental import pallas as pl
from jax.experimental.pallas import tpu as pltpu
from jax.sharding import PartitionSpec as P

MESH = pl.DeviceIdType.MESH
HD = 128
ROWS = 256
BLOCK = 320
Z = 8
QKV_ROWS, QKV_FIRST = 1120, 480
OUT_ROWS, OUT_FIRST = 800, 352
KEYS = 1024
NEG = -1e30
ROPE_THETA = 1000000.0
LOG2E = 1.4426950408889634
COPIES = 160


def dot(a, b):
    return lax.dot_general(a, b, (((1,), (0,)), ((), ())), preferred_element_type=jnp.float32)


def dot_t(a, b):
    return lax.dot_general(a, b, (((1,), (1,)), ((), ())), preferred_element_type=jnp.float32)


def kernel(
    h_hbm, wq_ref, wkv_ref, wo_ref, qb_ref, kvb_ref, prompt_hbm, par_ref, freq_ref, plen_ref,
    out_ref,
    hv, wbuf, obuf, pbuf, abuf, qx, qr, tk, tv, tsend, qs, reach_own, cosb, sinb,
    ss, rs, ls,
):
    j = lax.axis_index("ctx")
    i = lax.axis_index("smp")
    core = j % 2
    x = (j // 2) % 4
    yh = j // 8
    yl = i // Z
    z = i % Z
    head = j // 2
    sib = j + 1 - 2 * core
    other_y = (1 - yl) * Z + z

    def zat(d):
        return (z + d + Z) % Z

    counter = [0]
    started = []

    def new():
        counter[0] += 1
        return counter[0] - 1

    def send(k, src, dst, ctx, smp):
        copy = pltpu.make_async_remote_copy(
            src_ref=src, dst_ref=dst, send_sem=ss.at[k], recv_sem=rs.at[k],
            device_id={"ctx": ctx, "smp": smp}, device_id_type=MESH,
        )
        copy.start()
        started.append(copy)

    def landed(k, region):
        pltpu.make_async_copy(region, region, rs.at[k]).wait()

    barrier = pltpu.get_barrier_semaphore()
    for step in range(1, 16):
        pl.semaphore_signal(barrier, inc=1, device_id={"ctx": (j + step) % 16, "smp": i}, device_id_type=MESH)
    for smp in (yl * Z + zat(1), yl * Z + zat(-1), other_y):
        pl.semaphore_signal(barrier, inc=1, device_id={"ctx": j, "smp": smp}, device_id_type=MESH)
    for at in range(4):
        pl.semaphore_signal(
            barrier, inc=1, device_id={"ctx": ((1 - yh) * 4 + at) * 2 + core, "smp": other_y}, device_id_type=MESH
        )
    hcopy = pltpu.make_async_copy(h_hbm, hv, ls.at[0])
    hcopy.start()

    wq = wq_ref[...]
    main = jnp.where(core == 1, wq[:, 64:320], wq[:, 0:256])
    tail = jnp.where(core == 1, wq[:, 0:64], wq[:, 256:320])
    wbuf[i, 0:320, :] = main[:, 0:128]
    wbuf[i, 320:640, :] = main[:, 128:256]
    wbuf[i, 640:960, :] = wkv_ref[...]
    wbuf[i, 960:1120, :] = jnp.concatenate([tail[0:160], tail[160:320]], axis=1)
    pl.semaphore_wait(barrier, 22)

    class Gather:
        def __init__(self, buf, rows, first):
            self.buf, self.rows, self.first, self.half = buf, rows, first, rows // 2
            self.up = [new() for _ in range(4)]
            self.down = [new() for _ in range(4)]
            self.up2 = [new() for _ in range(4)]
            self.down2 = [new() for _ in range(4)]
            self.ya = new()
            self.yb = [new() for _ in range(8)]

        def at(self, y, d, lo, hi):
            return self.buf.at[y * Z + zat(d), pl.ds(lo, hi - lo), :]

        def ship(self, k, y, d, lo, hi, smp):
            region = self.at(y, d, lo, hi)
            send(k, region, region, j, smp)

        def start(self):
            self.ship(self.up[0], yl, 0, 0, self.rows, yl * Z + zat(1))
            self.ship(self.down[0], yl, 0, 0, self.rows, yl * Z + zat(-1))
            self.ship(self.ya, yl, 0, 0, self.first, other_y)
            self.ship(self.yb[0], yl, 0, self.first, self.rows, other_y)

        def start2(self):
            landed(self.ya, self.at(1 - yl, 0, 0, self.first))
            self.ship(self.up2[0], 1 - yl, 0, 0, self.first, yl * Z + zat(1))
            self.ship(self.down2[0], 1 - yl, 0, 0, self.first, yl * Z + zat(-1))

        def ring(self, s):
            last = s == 3
            mid = self.half if last else self.rows
            low = self.half if last else 0
            landed(self.up[s - 1], self.at(yl, -s, 0, self.rows))
            self.ship(self.up[s], yl, -s, 0, mid, yl * Z + zat(1))
            self.ship(self.yb[2 * s - 1], yl, -s, self.first, self.rows, other_y)
            landed(self.down[s - 1], self.at(yl, s, 0, self.rows))
            self.ship(self.down[s], yl, s, low, self.rows, yl * Z + zat(-1))
            self.ship(self.yb[2 * s], yl, s, self.first, self.rows, other_y)

        def ring2(self, s):
            last = s == 3
            mid = self.first // 2 if last else self.first
            low = self.first // 2 if last else 0
            landed(self.up2[s - 1], self.at(1 - yl, -s, 0, self.first))
            self.ship(self.up2[s], 1 - yl, -s, 0, mid, yl * Z + zat(1))
            landed(self.down2[s - 1], self.at(1 - yl, s, 0, self.first))
            self.ship(self.down2[s], 1 - yl, s, low, self.first, yl * Z + zat(-1))

        def far(self):
            landed(self.up[3], self.at(yl, 4, 0, self.half))
            landed(self.down[3], self.at(yl, 4, self.half, self.rows))
            self.ship(self.yb[7], yl, 4, self.first, self.rows, other_y)

        def finish(self):
            landed(self.up2[3], self.at(1 - yl, 4, 0, self.first // 2))
            landed(self.down2[3], self.at(1 - yl, 4, self.first // 2, self.first))
            for k, d in zip(self.yb, (0, -1, 1, -2, 2, -3, 3, 4)):
                landed(k, self.at(1 - yl, d, self.first, self.rows))

    gqkv = Gather(wbuf, QKV_ROWS, QKV_FIRST)
    gout = Gather(obuf, OUT_ROWS, OUT_FIRST)
    gqkv.start()

    own = pltpu.make_async_copy(prompt_hbm.at[head], pbuf.at[j], ls.at[1])
    own.start()
    row_k = [new() for _ in range(3)]
    cross_k = [new() for _ in range(4)]
    sib_k = [new() for _ in range(8)]
    for step in range(1, 4):
        to = yh * 4 + (x + step) % 4
        send(row_k[step - 1], prompt_hbm.at[to], pbuf.at[j], to * 2 + core, i)
    for step in range(4):
        to = (1 - yh) * 4 + (x + step) % 4
        send(cross_k[step], prompt_hbm.at[to], pbuf.at[j], to * 2 + core, other_y)
    send(sib_k[0], prompt_hbm.at[head], pbuf.at[j], sib, i)

    wo = wo_ref[...]
    obuf[i, 0:320, :] = wo[:, 0:128]
    obuf[i, 320:640, :] = wo[:, 128:256]
    obuf[i, 640:800, :] = jnp.concatenate([wo[0:160, 256:320], wo[160:320, 256:320]], axis=1)

    m_id = lax.broadcasted_iota(jnp.int32, (ROWS, ROWS), 0)
    n_id = lax.broadcasted_iota(jnp.int32, (ROWS, ROWS), 1)
    parent = par_ref[...] + (lax.broadcasted_iota(jnp.int32, (1, ROWS), 1) // 64) * 64
    hit = ((m_id == parent) & (n_id % 64 > 0)) | (m_id == n_id)
    reached = jnp.where(hit, 1.0, 0.0).astype(jnp.bfloat16)
    for _ in range(6):
        reached = jnp.minimum(dot(reached, reached), 1.0).astype(jnp.bfloat16)
    identity = jnp.where(m_id == n_id, 1.0, 0.0).astype(jnp.bfloat16)
    reach = dot_t(identity, reached)
    reach_own[...] = jnp.where(core == 0, reach[0:128, 0:128], reach[128:256, 128:256])
    row_id = lax.broadcasted_iota(jnp.int32, (ROWS, 1), 0)
    prefix = jnp.where(
        row_id < 128,
        jnp.where(row_id < 64, plen_ref[0], plen_ref[1]),
        jnp.where(row_id < 192, plen_ref[2], plen_ref[3]),
    ).astype(jnp.float32)
    positions = prefix + jnp.sum(reach, axis=1, keepdims=True) - 1.0
    angles = positions * freq_ref[...]
    lane = lax.broadcasted_iota(jnp.int32, (1, HD), 1)
    cosb[...] = jnp.cos(angles)
    sinb[...] = jnp.sin(angles) * jnp.where(lane < 64, -1.0, 1.0)

    def rope(v, cosine, sine):
        turned = jnp.concatenate([v[:, 64:128], v[:, 0:64]], axis=1)
        return v * cosine + turned * sine

    gqkv.start2()
    gqkv.ring(1)
    for step in range(1, 4):
        src = (yh * 4 + (x - step + 4) % 4) * 2 + core
        landed(row_k[step - 1], pbuf.at[src])
        send(sib_k[step], pbuf.at[src], pbuf.at[src], sib, i)
    gqkv.ring2(1)
    gqkv.ring(2)
    for step in range(4):
        src = ((1 - yh) * 4 + (x - step + 4) % 4) * 2 + core
        landed(cross_k[step], pbuf.at[src])
        send(sib_k[4 + step], pbuf.at[src], pbuf.at[src], sib, i)
    gqkv.ring2(2)
    gqkv.ring(3)
    gqkv.ring2(3)
    gqkv.far()
    gout.start()
    hcopy.wait()
    gqkv.finish()

    acc_q = jnp.zeros((ROWS, 256), jnp.float32)
    acc_r = jnp.zeros((ROWS, 192), jnp.float32)

    def project(p, carry):
        acc_q, acc_r = carry
        hk = hv[:, pl.ds(pl.multiple_of(p * 640, 128), 640)]
        wa, wb = wbuf.at[2 * p], wbuf.at[2 * p + 1]
        w_main = jnp.concatenate(
            [
                jnp.concatenate([wa[0:320, :], wa[320:640, :]], axis=1),
                jnp.concatenate([wb[0:320, :], wb[320:640, :]], axis=1),
            ],
            axis=0,
        )
        ta, tb = wa[960:1120, :], wb[960:1120, :]
        w_tail = jnp.concatenate([ta[:, 0:64], ta[:, 64:128], tb[:, 0:64], tb[:, 64:128]], axis=0)
        w_kv = jnp.concatenate([wa[640:960, :], wb[640:960, :]], axis=0)
        w_rest = jnp.concatenate([w_kv, w_tail], axis=1)
        return acc_q + dot(hk, w_main), acc_r + dot(hk, w_rest)

    acc_q, acc_r = lax.fori_loop(0, 8, project, (acc_q, acc_r))
    qb = qb_ref[...].astype(jnp.float32)
    qb_main = jnp.where(core == 1, qb[:, 64:320], qb[:, 0:256])
    qb_tail = jnp.where(core == 1, qb[:, 0:64], qb[:, 256:320])

    kv = (acc_r[:, 0:128] + kvb_ref[...].astype(jnp.float32)).astype(jnp.bfloat16)
    kvf = kv.astype(jnp.float32)
    tsend[...] = jnp.where(j < 8, rope(kvf, cosb[...], sinb[...]), kvf).astype(jnp.bfloat16)
    tree_k = [[new(), new()], [new(), new()]]
    for part, buf in ((0, tk), (1, tv)):
        for to_core in range(2):
            k = tree_k[part][to_core]
            to = (j % 8) * 2 + to_core
            src = tsend.at[pl.ds(to_core * 128, 128), :]

            @pl.when((j // 8 == part) & (to == j))
            def _():
                pltpu.make_async_copy(src, buf, rs.at[k]).start()

            @pl.when((j // 8 == part) & (to != j))
            def _():
                pltpu.make_async_remote_copy(
                    src_ref=src, dst_ref=buf, send_sem=ss.at[k], recv_sem=rs.at[k],
                    device_id={"ctx": to, "smp": i}, device_id_type=MESH,
                ).start()

    qx[:, 0:256] = (acc_q + qb_main).astype(jnp.bfloat16)
    qx[:, 256:384] = jnp.concatenate(
        [(acc_r[:, 128:192] + qb_tail).astype(jnp.bfloat16), jnp.zeros((ROWS, 64), jnp.bfloat16)], axis=1
    )
    qk = new()
    other_rows = pl.ds(pl.multiple_of((1 - core) * 128, 128), 128)
    own_rows = pl.ds(pl.multiple_of(core * 128, 128), 128)
    send(qk, qx.at[other_rows, :], qr, sib, i)
    gout.start2()
    gout.ring(1)
    landed(qk, qr)
    mine = qx[own_rows, :]
    theirs = qr[...]
    qa = jnp.where(core == 0, mine, theirs).astype(jnp.float32)
    qc = jnp.where(core == 0, theirs, mine).astype(jnp.float32)
    cosine, sine = cosb[own_rows, :], sinb[own_rows, :]
    heads = [
        qa[:, 0:128],
        qa[:, 128:256],
        jnp.concatenate([qa[:, 256:320], qc[:, 256:320]], axis=1),
        qc[:, 0:128],
        qc[:, 128:256],
    ]
    for g in range(5):
        rotated = rope(heads[g], cosine, sine).astype(jnp.bfloat16)
        for s in range(2):
            qs[s, g * 64 : (g + 1) * 64, :] = rotated[s * 64 : (s + 1) * 64, :]
    for to_core in range(2):

        @pl.when(core == to_core)
        def _():
            landed(tree_k[0][to_core], tk)
            landed(tree_k[1][to_core], tv)

    own.wait()
    for step in range(8):
        if step < 4:
            src = (yh * 4 + (x - step + 4) % 4) * 2 + 1 - core
        else:
            src = ((1 - yh) * 4 + (x - (step - 4) + 4) % 4) * 2 + 1 - core
        landed(sib_k[step], pbuf.at[src])

    factor = HD ** (-0.5) * LOG2E

    def attend(s):
        q = qs[s]
        allowed = jnp.concatenate([reach_own[s * 64 : (s + 1) * 64, :]] * 5, axis=0) > 0.5
        scores = jnp.where(allowed, dot_t(q, tk[...]) * factor, NEG)
        top = jnp.max(scores, axis=1, keepdims=True)
        weights = jnp.exp2(scores - top)
        total = jnp.sum(weights, axis=1, keepdims=True)
        acc = dot(weights.astype(jnp.bfloat16), tv[...])
        limit = jnp.where(core == 0, plen_ref[s], plen_ref[2 + s])

        def step(n, carry):
            top, total, acc = carry
            keys = pbuf[pl.ds(4 * n, 4), 0:256, :].reshape(KEYS, HD)
            values = pbuf[pl.ds(4 * n, 4), 256:512, :].reshape(KEYS, HD)
            at = lax.broadcasted_iota(jnp.int32, (1, KEYS), 1) + n * KEYS
            scores = jnp.where(at < limit, dot_t(q, keys) * factor, NEG)
            new_top = jnp.maximum(top, jnp.max(scores, axis=1, keepdims=True))
            weights = jnp.exp2(scores - new_top)
            shrink = jnp.exp2(top - new_top)
            total = total * shrink + jnp.sum(weights, axis=1, keepdims=True)
            acc = acc * shrink + dot(weights.astype(jnp.bfloat16), values)
            return new_top, total, acc

        top, total, acc = lax.fori_loop(0, 4, step, (top, total, acc))
        return (acc / total).astype(jnp.bfloat16)

    ab = [[new() for _ in range(15)] for _ in range(2)]
    opp = (1 - yh) * 4 + x

    def piece(h, c, s):
        return abuf.at[h, pl.ds(pl.multiple_of(c * 128 + s * 64, 64), 64), :]

    def spread(ks, region, s):
        for step in range(1, 4):
            send(ks[step - 1], region, region, (yh * 4 + (x + step) % 4) * 2 + core, i)
        send(ks[3], region, region, sib, i)

    for s in range(2):
        result = attend(s)
        for g in range(5):
            abuf[head, pl.ds(pl.multiple_of(core * 128 + s * 64, 64), 64), g * 128 : (g + 1) * 128] = result[
                g * 64 : (g + 1) * 64, :
            ]
        mine = piece(head, core, s)
        send(ab[s][14], mine, mine, opp * 2 + core, i)
        spread(ab[s][0:4], mine, s)
        gout.ring2(1 + s)
        gout.ring(2 + s)
    gout.ring2(3)
    gout.far()
    for s in range(2):
        theirs = piece(opp, core, s)
        landed(ab[s][14], theirs)
        spread(ab[s][4:8], theirs, s)
    for s in range(2):
        for row in range(2):
            for step in range(1, 4):
                at = (yh if row == 0 else 1 - yh) * 4 + (x - step + 4) % 4
                region = piece(at, core, s)
                landed(ab[s][4 * row + step - 1], region)
                send(ab[s][8 + 3 * row + step - 1], region, region, sib, i)
    gout.finish()
    for s in range(2):
        landed(ab[s][3], piece(head, 1 - core, s))
        landed(ab[s][7], piece(opp, 1 - core, s))
        for row in range(2):
            for step in range(1, 4):
                at = (yh if row == 0 else 1 - yh) * 4 + (x - step + 4) % 4
                landed(ab[s][8 + 3 * row + step - 1], piece(at, 1 - core, s))

    def combine(p, carry):
        acc_m, acc_t = carry
        wa, wb = obuf.at[2 * p], obuf.at[2 * p + 1]
        w_main = jnp.concatenate(
            [
                jnp.concatenate([wa[0:320, :], wa[320:640, :]], axis=1),
                jnp.concatenate([wb[0:320, :], wb[320:640, :]], axis=1),
            ],
            axis=0,
        )
        ta, tb = wa[640:800, :], wb[640:800, :]
        w_tail = jnp.concatenate([ta[:, 0:64], ta[:, 64:128], tb[:, 0:64], tb[:, 64:128]], axis=0)
        a = abuf[p]
        return acc_m + dot(a, w_main), acc_t + dot(a, w_tail)

    acc_m, acc_t = lax.fori_loop(
        0, 8, combine, (jnp.zeros((ROWS, 256), jnp.float32), jnp.zeros((ROWS, 64), jnp.float32))
    )
    out_ref[:, 0:256] = acc_m
    out_ref[:, 256:320] = acc_t

    for copy in started:
        copy.wait_send()
    for part in range(2):
        for to_core in range(2):
            k = tree_k[part][to_core]
            to = (j % 8) * 2 + to_core

            @pl.when((j // 8 == part) & (to != j))
            def _():
                src = tsend.at[pl.ds(to_core * 128, 128), :]
                pltpu.make_async_copy(src, src, ss.at[k]).wait()

    assert counter[0] <= COPIES, counter[0]


def shards(
    hidden_states, query_weight, kv_weight, out_weight, query_bias, kv_bias, prompt_kv, parents, prefix_len
):
    prompt = prompt_kv.reshape(256, 2, 8, HD).transpose(2, 1, 0, 3).reshape(8, 512, HD)
    frequency = ROPE_THETA ** (-jnp.arange(64, dtype=jnp.float32) / 64)
    frequency = jnp.tile(frequency, 2).reshape(1, HD)
    vmem = pl.BlockSpec(memory_space=pltpu.VMEM)
    anywhere = pl.BlockSpec(memory_space=pl.ANY)
    b16 = jnp.bfloat16
    out = pl.pallas_call(
        kernel,
        out_shape=jax.ShapeDtypeStruct((ROWS, BLOCK), jnp.float32),
        in_specs=[anywhere, vmem, vmem, vmem, vmem, vmem, anywhere, vmem, vmem, pl.BlockSpec(memory_space=pltpu.SMEM)],
        out_specs=vmem,
        scratch_shapes=[
            pltpu.VMEM((ROWS, 5120), b16),
            pltpu.VMEM((16, QKV_ROWS, 128), b16),
            pltpu.VMEM((16, OUT_ROWS, 128), b16),
            pltpu.VMEM((16, 512, 128), b16),
            pltpu.VMEM((8, ROWS, 640), b16),
            pltpu.VMEM((ROWS, 384), b16),
            pltpu.VMEM((128, 384), b16),
            pltpu.VMEM((128, 128), b16),
            pltpu.VMEM((128, 128), b16),
            pltpu.VMEM((ROWS, 128), b16),
            pltpu.VMEM((2, 320, 128), b16),
            pltpu.VMEM((128, 128), jnp.float32),
            pltpu.VMEM((ROWS, 128), jnp.float32),
            pltpu.VMEM((ROWS, 128), jnp.float32),
            pltpu.SemaphoreType.DMA((COPIES,)),
            pltpu.SemaphoreType.DMA((COPIES,)),
            pltpu.SemaphoreType.DMA((2,)),
        ],
        compiler_params=pltpu.CompilerParams(
            collective_id=0, has_side_effects=True, vmem_limit_bytes=56 * 1024 * 1024
        ),
    )(
        hidden_states.reshape(ROWS, 5120), query_weight, kv_weight, out_weight, query_bias.reshape(1, BLOCK),
        kv_bias.reshape(1, HD), prompt, parents.reshape(1, ROWS), frequency, prefix_len,
    )
    return out.reshape(4, 64, BLOCK)


def solution(mesh):
    return jax.shard_map(
        shards,
        mesh=mesh,
        in_specs=(
            P("smp", None, None),
            P("smp", "ctx"),
            P("smp", "ctx"),
            P("smp", "ctx"),
            P("ctx"),
            P("ctx"),
            P("ctx", None, None),
            P("smp", None),
            P("smp"),
        ),
        out_specs=P("smp", None, "ctx"),
        check_vma=False,
    )
```

time: 661 us -> 99.3 us (0.15)
  waiting for transfers between devices: 515 us -> 0 us
  Pallas kernels: 0 us -> 92.4 us
  local copies, waits for them, and re-layouts: 67.6 us -> 6.68 us
  matrix products: 25.5 us -> 0 us
  starting transfers between devices: 22.7 us -> 0 us
  other arithmetic: 14.6 us -> 0.01 us
  between operations: 13.5 us -> 0.02 us
    ppermute x15 -> x0, waiting for transfers between devices: 264 us -> none  [passed_along(): return lax.ppermute(block, axis, route)]
    all_gather x5 -> x0, waiting for transfers between devices: 241 us -> none  [the longest x1 65.1 us: shards(): lax.all_gather(kv_weight, 'smp', axis=0, tiled=True)]
    pallas_call x0 -> x1, Pallas kernels: none -> 92.4 us  [shards(): pl.pallas_call(kernel, out_shape=jax.ShapeDtypeStruct((ROWS, BLOCK), jnp....]
    while x31 -> x0, local copies, waits for them, and re-layouts: 38.7 us -> none
    dot_general x43 -> x0, matrix products: 25.5 us -> none  [the longest x17 6.52 us: attend_block(): jnp.einsum('rkgp,pkd->rkgd', weights.astype(jnp.bfloat16), values, prefer...]
    slice x17 -> x0, local copies, waits for them, and re-layouts: 22.9 us -> none  [the longest x16 21.3 us: split_block(): block[:, 1].reshape(block.shape[0], heads_here, HD)]
    all_to_all x1 -> x0, starting transfers between devices: 15.8 us -> none  [shards(): lax.all_to_all(query_part, 'ctx', split_axis=0, concat_axis=1, tiled=True)]
    all_to_all x1 -> x0, waiting for transfers between devices: 8.08 us -> none  [shards(): lax.all_to_all(query_part, 'ctx', split_axis=0, concat_axis=1, tiled=True)]
  transfers between devices with their start and end apart: 21 -> 0, of which waited for: 20 -> 0; matrix products, arithmetic and copies ran while one was open for 15% -> 0% of each run, Pallas kernels for 0% -> 0%
where the time goes in v1:
time: 99.3 us; the launch traced here: 99.1 us
  Pallas kernels  92.4 us (93%)
  local copies, waits for them, and re-layouts  6.68 us (7%)
    pallas_call x1, Pallas kernels, shards(): pl.pallas_call(kernel, out_shape=jax.ShapeDtypeStruct((ROWS, BLOCK), jnp....  92.4 us
    reshape x2, local copies, waits for them, and re-layouts, shards(): prompt_kv.reshape(256, 2, 8, HD).transpose(2, 1, 0, 3).reshape(8, 512, HD)  3.01 us

profile of v1, /device:TPU:1, one launch (start us, length us, event | category | flops | bytes accessed | tf_op | source)
XLA Modules:
  0.0 99.1 jit_solution(8348854726205723585)
XLA Ops:
  0.0 0.0 copy-start.1
  0.0 0.0 copy-start
  0.0 1.8 %reshape.30 = bf16[256,2,8,128]{3,2,1,0:T(8,128)(2,1)S(1)} reshape(bf16[256,2,1024]{2,1,0:T(2,128)(2,1)} %param.15) | data formatting | bytes 2097152 | tf_op jit(solution)/shard_map/reshape | solution.py:417
  1.8 1.2 %copy.10 = bf16[256,2,8,128]{3,0,1,2:T(8,128)(2,1)} copy(bf16[256,2,8,128]{3,2,1,0:T(8,128)(2,1)S(1)} %reshape.30) | data formatting | bytes 2097152 | tf_op jit(solution)/shard_map/reshape | solution.py:417
  3.0 0.7 reshape_tile.3.freq_ref
  3.7 0.0 copy-done.1
  3.7 0.6 reshape.28.qb_ref
  4.3 0.0 copy-done
  4.3 0.7 reshape.32.par_ref
  4.9 92.4 %shard_map.91 = f32[256,320]{1,0:T(8,128)} custom-call(bf16[256,5120]{1,0:T(8,128)(2,1)} %bitcast.7, bf16[320,320]{1,0:T(8,128)(2,1)} %wq_ref.1, bf16[320,128]{1,0:T(8,128)(2,1)} %wkv_ref.1, bf16[320,320]{1,0:T(8,128)(2,1)} %wo_ref.1, bf16[1,320]{1,0:T(2,128)(2,1)} %reshape.28.qb_ref, bf16[1,128]{1,0:T(2,128)(2,1)} %bitcast.9, bf16[8,512,128]{2,1,0:T(8,128)(2,1)} %bitcast.6, ...), custom_call_target="tpu_custom_call" | custom-call | tf_op jit(solution)/shard_map/pallas_call | solution.py:423
  97.4 1.8 %copy.12 = f32[4,64,320]{2,1,0:T(8,128)} copy(f32[4,64,320]{2,1,0:T(8,128)} %bitcast.8) | data formatting | bytes 655360
  (2 shorter events, 0.0 us)
Async XLA Ops:
  0.0 3.7 %copy-start.1 = (bf16[320]{0:T(512)(128)(2,1)S(1)}, bf16[320]{0:T(512)(128)(2,1)}, u32[]{:S(2)}) copy-start(bf16[320]{0:T(512)(128)(2,1)} %param.13) | copy-start | bytes 1924
  0.0 4.3 %copy-start = (s32[4,64]{1,0:T(4,128)S(1)}, s32[4,64]{1,0:T(4,128)}, u32[]{:S(2)}) copy-start(s32[4,64]{1,0:T(4,128)} %param.16) | copy-start | bytes 3076
